TPU v7x, 512 devices: a whole 4x8x8 slice. The times are simulated.
512 devices in a mesh: ctx: 128 (over z_lo, y, x), tp: 4 (over z_hi, core).
Axes of the slice: x: 4, y: 8, z: 8 (z_hi: 2, z_lo: 4; z = z_hi * 4 + z_lo), core: 2. Of those that a mesh axis runs over, the one named last changes fastest.
Arguments:
- hyena_inputs: bfloat16 [3, 16384, 4096], P(None, 'ctx', 'tp'), may hold values from -6 to 6
- filters: float32 [128, 4096], P('tp'), may hold values from -1.25 to 1.25
- skip_bias: float32 [4096], P('tp'), may hold values from -4 to 4
- queries: bfloat16 [16384, 4096], P('ctx', 'tp'), may hold values from -8 to 8
- keys_values: bfloat16 [2, 16384, 4096], P(None, 'ctx', 'tp'), may hold values from -8 to 8
- doc_start: int32 [16384], P('ctx'), may hold values from 0 to 16383, as said below
Outputs:
- hyena_out: bfloat16 [16384, 4096], P('ctx', 'tp')
- attention_out: bfloat16 [16384, 4096], P('ctx', 'tp')
- log_totals: float32 [32, 16384], P('tp', 'ctx')
Inputs may be any that keep to these rules, and one draw needn't show every extreme that they name: doc_start[t] <= t; doc_start is non-decreasing, equal within a document and equal to t at a document's first base; no document is longer than 896 bases and one has exactly 896; the last base forms a document of its own.
All inputs are finite; a program needn't handle non-finite values.
Results may differ from a plain program's by a relative error of at most 0.009.
Values may be sent and summed in bfloat16 or wider, within the bound.
A program may use at most 128 MiB of HBM per device.

v0:
```python
import math

import jax
import jax.numpy as jnp
from jax import lax
from jax.sharding import PartitionSpec as P

HD = 128
FLEN = 128
HOPS = 7


def shifted_2(shard, axis, by):
    peers = lax.axis_size(axis)
    pairs = [(i, i + by) for i in range(peers) if 0 <= i + by < peers]
    return lax.ppermute(shard, axis, pairs)


def local(hyena_inputs, filters, skip_bias, queries, keys_values, doc_start):
    row_count = hyena_inputs.shape[1]
    cycle_index = lax.axis_index("ctx")
    first_row = cycle_index * row_count
    places = first_row + jnp.arange(row_count, dtype=jnp.int32)
    kv_product = (hyena_inputs[1].astype(jnp.float32) * hyena_inputs[2].astype(jnp.float32)).astype(
        jnp.bfloat16
    )
    panel_taps = lax.all_to_all(
        filters.astype(jnp.bfloat16), "tp", split_axis=1, concat_axis=0, tiled=True
    ).astype(filters.dtype)
    left_rim = shifted_2(kv_product[row_count - (FLEN - 1) :], "ctx", 1)
    extended = jnp.concatenate([left_rim, kv_product], axis=0)
    channel_count = kv_product.shape[1]
    reach = (places - doc_start)[:, None]
    convolved = jnp.zeros((row_count, channel_count), jnp.float32)
    for lag in range(FLEN):
        shifted = extended[FLEN - 1 - lag : FLEN - 1 - lag + row_count].astype(jnp.float32)
        convolved = convolved + jnp.where(reach >= lag, shifted * panel_taps[lag][None, :], 0.0)
    hyena_out = (
        hyena_inputs[0].astype(jnp.float32)
        * (skip_bias[None, :] * kv_product.astype(jnp.float32) + convolved)
    ).astype(jnp.bfloat16)
    head_count = queries.shape[1] // HD
    query_heads = queries.reshape(row_count, head_count, HD)
    score_scale = 1.0 / math.sqrt(HD)
    pieces = [keys_values]
    for distance in range(1, HOPS + 1):
        pieces.append(shifted_2(pieces[-1], "ctx", 1))
    carried = (
        jnp.full((head_count, row_count), -jnp.inf, jnp.float32),
        jnp.zeros((head_count, row_count), jnp.float32),
        jnp.zeros((head_count, row_count, HD), jnp.float32),
    )
    for pair_index in range((HOPS + 1) // 2):
        block = jnp.concatenate([pieces[2 * pair_index + 1], pieces[2 * pair_index]], axis=1)
        key_first = (cycle_index - 2 * pair_index - 1) * row_count
        add_row_top, add_denominator, add_accumulated = carried
        key_rows = block[0].reshape(2 * row_count, head_count, HD)
        value_rows = block[1].reshape(2 * row_count, head_count, HD)
        scores = (
            jnp.einsum("thd,khd->htk", query_heads, key_rows, preferred_element_type=jnp.float32)
            * score_scale
        )
        key_places = key_first + jnp.arange(2 * row_count, dtype=jnp.int32)
        allowed = (key_places[None, :] >= doc_start[:, None]) & (
            key_places[None, :] <= places[:, None]
        )
        scores = jnp.where(allowed[None], scores, -jnp.inf)
        new_top = jnp.maximum(add_row_top, jnp.max(scores, axis=2))
        weights = jnp.exp(scores - new_top[:, :, None])
        rescale = jnp.exp(add_row_top - new_top)
        add_denominator = add_denominator * rescale + jnp.sum(weights, axis=2)
        add_accumulated = add_accumulated * rescale[:, :, None] + jnp.einsum(
            "htk,khd->htd",
            weights.astype(jnp.bfloat16),
            value_rows,
            preferred_element_type=jnp.float32,
        )
        carried = (new_top, add_denominator, add_accumulated)
    row_top, denominator, accumulated = carried
    attention_out = (
        (accumulated / denominator[:, :, None])
        .transpose(1, 0, 2)
        .reshape(row_count, head_count * HD)
        .astype(jnp.bfloat16)
    )
    log_totals = row_top + jnp.log(denominator)
    return (hyena_out, attention_out, log_totals)


def solution(mesh):
    in_specs = (
        P(None, "ctx", "tp"),
        P("tp", None),
        P("tp"),
        P("ctx", "tp"),
        P(None, "ctx", "tp"),
        P("ctx"),
    )
    out_specs = (P("ctx", "tp"), P("ctx", "tp"), P("tp", "ctx"))
    return jax.shard_map(local, mesh=mesh, in_specs=in_specs, out_specs=out_specs, check_vma=False)
```

profile of v0, /device:TPU:64, one launch (start us, length us, event | category | flops | bytes accessed | tf_op | source)
XLA Modules:
  0.0 279.1 jit_solution(9899110803998919781)
XLA Ops:
  0.7 1.2 convert_element_type.445
  1.8 0.7 copy.104
  2.5 9.4 %all-to-all-start = ((bf16[32,4,1024]{2,0,1:T(8,128)(2,1)}), bf16[32,4,1024]{2,0,1:T(8,128)(2,1)}, u32[]{:S(2)}, u32[]{:S(2)}) async-start(bf16[32,4,1024]{2,0,1:T(8,128)(2,1)} %bitcast.294), calls=%async_computation | async-start | bytes 524288 | tf_op jit(solution)/shard_map/all_to_all | solution.py:27
  12.1 3.5 %collective-permute-start = (bf16[127,1024]{1,0:T(8,128)(2,1)S(1)}, bf16[127,1024]{1,0:T(8,128)(2,1)S(1)}, u32[]{:S(2)}, u32[]{:S(2)}) collective-permute-start(bf16[127,1024]{1,0:T(8,128)(2,1)S(1)} %slice_bitcast_fusion), channel_id=1, source_target_pairs={{0,4},{4,8},{8,12},{12,16},{16,20},{20,24},{24,28},{28,32},{32,36}... | collective-permute-start | bytes 780296 | tf_op jit(solution)/shard_map/ppermute | solution.py:16
  15.9 3.4 %collective-permute-start.1 = (bf16[2,128,1024]{1,2,0:T(8,128)(2,1)S(1)}, bf16[2,128,1024]{1,2,0:T(8,128)(2,1)}, u32[]{:S(2)}, u32[]{:S(2)}) collective-permute-start(bf16[2,128,1024]{1,2,0:T(8,128)(2,1)S(1)} %copy.54), channel_id=1, source_target_pairs={{0,4},{4,8},{8,12},{12,16},{16,20},{20,24},{24,28},{28,32},{32,36}... | collective-permute-start | bytes 1572872 | tf_op jit(solution)/shard_map/ppermute | solution.py:16
  19.3 0.6 copy-done.43
  20.7 1.5 broadcast_compare_fusion.81
  22.3 7.7 %collective-permute-done = bf16[127,1024]{1,0:T(8,128)(2,1)S(1)} collective-permute-done((bf16[127,1024]{1,0:T(8,128)(2,1)S(1)}, bf16[127,1024]{1,0:T(8,128)(2,1)S(1)}, u32[]{:S(2)}, u32[]{:S(2)}) %collective-permute-start) | collective-permute-done | bytes 260128 | tf_op jit(solution)/shard_map/ppermute | solution.py:16
  30.0 1.5 fusion.107
  31.4 1.5 fusion.179
  33.0 1.6 fusion.152
  34.6 1.6 fusion.170
  36.2 1.6 fusion.161
  37.7 1.6 fusion.134
  39.4 1.5 fusion.116
  40.9 1.6 fusion.125
  42.5 1.6 fusion.143
  44.2 1.1 convert_element_type.585
  45.4 1.9 collective-permute-start.2
  47.6 17.0 %collective-permute-done.2 = bf16[2,128,1024]{1,2,0:T(8,128)(2,1)S(1)} collective-permute-done((bf16[2,128,1024]{1,2,0:T(8,128)(2,1)}, bf16[2,128,1024]{1,2,0:T(8,128)(2,1)S(1)}, u32[]{:S(2)}, u32[]{:S(2)}) %collective-permute-start.2) | collective-permute-done | bytes 524320 | tf_op jit(solution)/shard_map/ppermute | solution.py:16
  64.6 1.9 collective-permute-start.3
  67.1 15.6 %collective-permute-done.3 = bf16[2,128,1024]{1,2,0:T(8,128)(2,1)S(1)} collective-permute-done((bf16[2,128,1024]{1,2,0:T(8,128)(2,1)S(1)}, bf16[2,128,1024]{1,2,0:T(8,128)(2,1)S(1)}, u32[]{:S(2)}, u32[]{:S(2)}) %collective-permute-start.3) | collective-permute-done | bytes 524320 | tf_op jit(solution)/shard_map/ppermute | solution.py:16
  82.7 1.9 collective-permute-start.4
  85.7 139.6 %fusion.27 = bf16[128,1024]{1,0:T(8,128)(2,1)} fusion(bf16[128,1024]{1,0:T(8,128)(2,1)S(1)} %get-tuple-element.242, bf16[128,1024]{1,0:T(8,128)(2,1)S(1)} %get-tuple-element.241, bf16[128,1024]{1,0:T(8,128)(2,1)} %get-tuple-element.240, bf16[128,1024]{1,0:T(8,128)(2,1)} %get-tuple-element.239, bf16[128,1024]{1,0:T(8,128)(2,1)S(1)} %copy-done.15, ...), kind=kLoop, calls=%fused_computation.295 | loop fusion | flops 84279296 | bytes 24131456 | tf_op jit(solution)/shard_map/convert_element_type | solution.py:41
  225.3 1.1 fusion.57
  226.4 1.9 collective-permute-start.5
  229.2 14.4 %collective-permute-done.5 = bf16[2,128,1024]{1,2,0:T(8,128)(2,1)S(1)} collective-permute-done((bf16[2,128,1024]{1,2,0:T(8,128)(2,1)S(1)}, bf16[2,128,1024]{1,2,0:T(8,128)(2,1)S(1)}, u32[]{:S(2)}, u32[]{:S(2)}) %collective-permute-start.5) | collective-permute-done | bytes 524320 | tf_op jit(solution)/shard_map/ppermute | solution.py:16
  243.6 1.9 collective-permute-start.6
  246.2 13.6 %collective-permute-done.6 = bf16[2,128,1024]{1,2,0:T(8,128)(2,1)S(1)} collective-permute-done((bf16[2,128,1024]{1,2,0:T(8,128)(2,1)S(1)}, bf16[2,128,1024]{1,2,0:T(8,128)(2,1)S(1)}, u32[]{:S(2)}, u32[]{:S(2)}) %collective-permute-start.6) | collective-permute-done | bytes 524320 | tf_op jit(solution)/shard_map/ppermute | solution.py:16
  259.8 2.1 collective-permute-start.7
  262.3 12.7 %collective-permute-done.7 = bf16[2,128,1024]{1,2,0:T(8,128)(2,1)S(1)} collective-permute-done((bf16[2,128,1024]{1,2,0:T(8,128)(2,1)S(1)}, bf16[2,128,1024]{1,2,0:T(8,128)(2,1)S(1)}, u32[]{:S(2)}, u32[]{:S(2)}) %collective-permute-start.7) | collective-permute-done | bytes 524320 | tf_op jit(solution)/shard_map/ppermute | solution.py:16
  278.2 0.9 copy.68
  (132 shorter events, 7.6 us)
Async XLA Ops:
  0.6 227.8 %copy-start = (bf16[128,1024]{1,0:T(8,128)(2,1)S(1)}, bf16[128,1024]{1,0:T(8,128)(2,1)}, u32[]{:S(2)}) copy-start(bf16[128,1024]{1,0:T(8,128)(2,1)} %param.9) | copy-start | bytes 786436
  2.5 41.6 %all-to-all-start = ((bf16[32,4,1024]{2,0,1:T(8,128)(2,1)}), bf16[32,4,1024]{2,0,1:T(8,128)(2,1)}, u32[]{:S(2)}, u32[]{:S(2)}) async-start(bf16[32,4,1024]{2,0,1:T(8,128)(2,1)} %bitcast.294), calls=%async_computation | async-start | bytes 524288 | tf_op jit(solution)/shard_map/all_to_all | solution.py:27
  12.1 17.9 %collective-permute-start = (bf16[127,1024]{1,0:T(8,128)(2,1)S(1)}, bf16[127,1024]{1,0:T(8,128)(2,1)S(1)}, u32[]{:S(2)}, u32[]{:S(2)}) collective-permute-start(bf16[127,1024]{1,0:T(8,128)(2,1)S(1)} %slice_bitcast_fusion), channel_id=1, source_target_pairs={{0,4},{4,8},{8,12},{12,16},{16,20},{20,24},{24,28},{28,32},{32,36}... | collective-permute-start | bytes 780296 | tf_op jit(solution)/shard_map/ppermute | solution.py:16
  15.9 29.5 %collective-permute-start.1 = (bf16[2,128,1024]{1,2,0:T(8,128)(2,1)S(1)}, bf16[2,128,1024]{1,2,0:T(8,128)(2,1)}, u32[]{:S(2)}, u32[]{:S(2)}) collective-permute-start(bf16[2,128,1024]{1,2,0:T(8,128)(2,1)S(1)} %copy.54), channel_id=1, source_target_pairs={{0,4},{4,8},{8,12},{12,16},{16,20},{20,24},{24,28},{28,32},{32,36}... | collective-permute-start | bytes 1572872 | tf_op jit(solution)/shard_map/ppermute | solution.py:16
  44.2 40.5 %copy-start.13 = (bf16[128,1024]{1,0:T(8,128)(2,1)S(1)}, bf16[128,1024]{1,0:T(8,128)(2,1)}, u32[]{:S(2)}) copy-start(bf16[128,1024]{1,0:T(8,128)(2,1)} %get-tuple-element.236) | copy-start | bytes 786436
  44.2 40.5 %copy-start.14 = (bf16[128,1024]{1,0:T(8,128)(2,1)S(1)}, bf16[128,1024]{1,0:T(8,128)(2,1)}, u32[]{:S(2)}) copy-start(bf16[128,1024]{1,0:T(8,128)(2,1)} %get-tuple-element.237) | copy-start | bytes 786436
  44.2 40.5 %copy-start.15 = (bf16[128,1024]{1,0:T(8,128)(2,1)S(1)}, bf16[128,1024]{1,0:T(8,128)(2,1)}, u32[]{:S(2)}) copy-start(bf16[128,1024]{1,0:T(8,128)(2,1)} %get-tuple-element.238) | copy-start | bytes 786436
  45.3 39.4 %copy-start.12 = (bf16[128,1024]{1,0:T(8,128)(2,1)S(1)}, bf16[128,1024]{1,0:T(8,128)(2,1)}, u32[]{:S(2)}) copy-start(bf16[128,1024]{1,0:T(8,128)(2,1)} %get-tuple-element.235) | copy-start | bytes 786436
  45.4 19.2 %collective-permute-start.2 = (bf16[2,128,1024]{1,2,0:T(8,128)(2,1)}, bf16[2,128,1024]{1,2,0:T(8,128)(2,1)S(1)}, u32[]{:S(2)}, u32[]{:S(2)}) collective-permute-start(bf16[2,128,1024]{1,2,0:T(8,128)(2,1)} %collective-permute-done.1), channel_id=1, source_target_pairs={{0,4},{4,8},{8,12},{12,16},{16,20},{20,24},{24,28},{28,32},{32,36}... | collective-permute-start | bytes 1572872 | tf_op jit(solution)/shard_map/ppermute | solution.py:16
  47.3 37.3 %copy-start.11 = (bf16[128,1024]{1,0:T(8,128)(2,1)S(1)}, bf16[128,1024]{1,0:T(8,128)(2,1)}, u32[]{:S(2)}) copy-start(bf16[128,1024]{1,0:T(8,128)(2,1)} %get-tuple-element.234) | copy-start | bytes 786436
  47.5 19.2 %copy-start.42 = (pred[128]{0:T(512)(128)(4,1)S(1)}, pred[128]{0:T(512)(128)(4,1)}, u32[]{:S(2)}) copy-start(pred[128]{0:T(512)(128)(4,1)} %get-tuple-element.330) | copy-start | bytes 388
  47.5 37.2 %copy-start.10 = (bf16[128,1024]{1,0:T(8,128)(2,1)S(1)}, bf16[128,1024]{1,0:T(8,128)(2,1)}, u32[]{:S(2)}) copy-start(bf16[128,1024]{1,0:T(8,128)(2,1)} %get-tuple-element.233) | copy-start | bytes 786436
  64.6 18.1 %collective-permute-start.3 = (bf16[2,128,1024]{1,2,0:T(8,128)(2,1)S(1)}, bf16[2,128,1024]{1,2,0:T(8,128)(2,1)S(1)}, u32[]{:S(2)}, u32[]{:S(2)}) collective-permute-start(bf16[2,128,1024]{1,2,0:T(8,128)(2,1)S(1)} %collective-permute-done.2), channel_id=1, source_target_pairs={{0,4},{4,8},{8,12},{12,16},{16,20},{20,24},{24,28},{28,32},{32,36}... | collective-permute-start | bytes 1572872 | tf_op jit(solution)/shard_map/ppermute | solution.py:16
  66.6 18.1 %copy-start.9 = (bf16[128,1024]{1,0:T(8,128)(2,1)S(1)}, bf16[128,1024]{1,0:T(8,128)(2,1)}, u32[]{:S(2)}) copy-start(bf16[128,1024]{1,0:T(8,128)(2,1)} %get-tuple-element.232) | copy-start | bytes 786436
  66.7 18.0 %copy-start.5 = (bf16[128,1024]{1,0:T(8,128)(2,1)S(1)}, bf16[128,1024]{1,0:T(8,128)(2,1)}, u32[]{:S(2)}) copy-start(bf16[128,1024]{1,0:T(8,128)(2,1)} %get-tuple-element.165) | copy-start | bytes 786436
  66.7 18.0 %copy-start.6 = (bf16[128,1024]{1,0:T(8,128)(2,1)S(1)}, bf16[128,1024]{1,0:T(8,128)(2,1)}, u32[]{:S(2)}) copy-start(bf16[128,1024]{1,0:T(8,128)(2,1)} %get-tuple-element.166) | copy-start | bytes 786436
  66.7 18.0 %copy-start.7 = (bf16[128,1024]{1,0:T(8,128)(2,1)S(1)}, bf16[128,1024]{1,0:T(8,128)(2,1)}, u32[]{:S(2)}) copy-start(bf16[128,1024]{1,0:T(8,128)(2,1)} %get-tuple-element.167) | copy-start | bytes 786436
  66.7 18.0 %copy-start.8 = (bf16[128,1024]{1,0:T(8,128)(2,1)S(1)}, bf16[128,1024]{1,0:T(8,128)(2,1)}, u32[]{:S(2)}) copy-start(bf16[128,1024]{1,0:T(8,128)(2,1)} %get-tuple-element.168) | copy-start | bytes 786436
  66.7 18.0 %copy-start.17 = (f32[1024]{0:T(1024)S(1)}, f32[1024]{0:T(1024)}, u32[]{:S(2)}) copy-start(f32[1024]{0:T(1024)} %param.8) | copy-start | bytes 12292
  66.7 18.0 %copy-start.18 = (pred[128]{0:T(512)(128)(4,1)S(1)}, pred[128]{0:T(512)(128)(4,1)}, u32[]{:S(2)}) copy-start(pred[128]{0:T(512)(128)(4,1)} %get-tuple-element.252) | copy-start | bytes 388
  66.7 18.0 %copy-start.19 = (pred[128]{0:T(512)(128)(4,1)S(1)}, pred[128]{0:T(512)(128)(4,1)}, u32[]{:S(2)}) copy-start(pred[128]{0:T(512)(128)(4,1)} %get-tuple-element.253) | copy-start | bytes 388
  66.7 18.0 %copy-start.20 = (pred[128]{0:T(512)(128)(4,1)S(1)}, pred[128]{0:T(512)(128)(4,1)}, u32[]{:S(2)}) copy-start(pred[128]{0:T(512)(128)(4,1)} %get-tuple-element.254) | copy-start | bytes 388
  66.8 18.0 %copy-start.21 = (pred[128]{0:T(512)(128)(4,1)S(1)}, pred[128]{0:T(512)(128)(4,1)}, u32[]{:S(2)}) copy-start(pred[128]{0:T(512)(128)(4,1)} %get-tuple-element.255) | copy-start | bytes 388
  66.8 18.0 %copy-start.22 = (pred[128]{0:T(512)(128)(4,1)S(1)}, pred[128]{0:T(512)(128)(4,1)}, u32[]{:S(2)}) copy-start(pred[128]{0:T(512)(128)(4,1)} %get-tuple-element.256) | copy-start | bytes 388
  66.8 18.0 %copy-start.23 = (pred[128]{0:T(512)(128)(4,1)S(1)}, pred[128]{0:T(512)(128)(4,1)}, u32[]{:S(2)}) copy-start(pred[128]{0:T(512)(128)(4,1)} %get-tuple-element.257) | copy-start | bytes 388
  66.8 18.0 %copy-start.24 = (pred[128]{0:T(512)(128)(4,1)S(1)}, pred[128]{0:T(512)(128)(4,1)}, u32[]{:S(2)}) copy-start(pred[128]{0:T(512)(128)(4,1)} %get-tuple-element.258) | copy-start | bytes 388
  66.8 18.0 %copy-start.25 = (pred[128]{0:T(512)(128)(4,1)S(1)}, pred[128]{0:T(512)(128)(4,1)}, u32[]{:S(2)}) copy-start(pred[128]{0:T(512)(128)(4,1)} %get-tuple-element.259) | copy-start | bytes 388
  66.8 18.0 %copy-start.26 = (pred[128]{0:T(512)(128)(4,1)S(1)}, pred[128]{0:T(512)(128)(4,1)}, u32[]{:S(2)}) copy-start(pred[128]{0:T(512)(128)(4,1)} %get-tuple-element.260) | copy-start | bytes 388
  82.7 143.8 %collective-permute-start.4 = (bf16[2,128,1024]{1,2,0:T(8,128)(2,1)S(1)}, bf16[2,128,1024]{1,2,0:T(8,128)(2,1)S(1)}, u32[]{:S(2)}, u32[]{:S(2)}) collective-permute-start(bf16[2,128,1024]{1,2,0:T(8,128)(2,1)S(1)} %collective-permute-done.3), channel_id=1, source_target_pairs={{0,4},{4,8},{8,12},{12,16},{16,20},{20,24},{24,28},{28,32},{32,36}... | collective-permute-start | bytes 1572872 | tf_op jit(solution)/shard_map/ppermute | solution.py:16
  226.4 17.1 %collective-permute-start.5 = (bf16[2,128,1024]{1,2,0:T(8,128)(2,1)S(1)}, bf16[2,128,1024]{1,2,0:T(8,128)(2,1)S(1)}, u32[]{:S(2)}, u32[]{:S(2)}) collective-permute-start(bf16[2,128,1024]{1,2,0:T(8,128)(2,1)S(1)} %collective-permute-done.4), channel_id=1, source_target_pairs={{0,4},{4,8},{8,12},{12,16},{16,20},{20,24},{24,28},{28,32},{32,36}... | collective-permute-start | bytes 1572872 | tf_op jit(solution)/shard_map/ppermute | solution.py:16
  243.6 16.2 %collective-permute-start.6 = (bf16[2,128,1024]{1,2,0:T(8,128)(2,1)S(1)}, bf16[2,128,1024]{1,2,0:T(8,128)(2,1)S(1)}, u32[]{:S(2)}, u32[]{:S(2)}) collective-permute-start(bf16[2,128,1024]{1,2,0:T(8,128)(2,1)S(1)} %collective-permute-done.5), channel_id=1, source_target_pairs={{0,4},{4,8},{8,12},{12,16},{16,20},{20,24},{24,28},{28,32},{32,36}... | collective-permute-start | bytes 1572872 | tf_op jit(solution)/shard_map/ppermute | solution.py:16
  259.8 15.3 %collective-permute-start.7 = (bf16[2,128,1024]{1,2,0:T(8,128)(2,1)S(1)}, bf16[2,128,1024]{1,2,0:T(8,128)(2,1)S(1)}, u32[]{:S(2)}, u32[]{:S(2)}) collective-permute-start(bf16[2,128,1024]{1,2,0:T(8,128)(2,1)S(1)} %collective-permute-done.6), channel_id=1, source_target_pairs={{0,4},{4,8},{8,12},{12,16},{16,20},{20,24},{24,28},{28,32},{32,36}... | collective-permute-start | bytes 1572872 | tf_op jit(solution)/shard_map/ppermute | solution.py:16
  (21 other events, 288.9 us)
where the time goes:
time: 280 us; the launch traced here: 279 us
  other arithmetic  161 us (58%)
  waiting for transfers between devices  81.1 us (29%)
  starting transfers between devices  28 us (10%)
  local copies, waits for them, and re-layouts  4.72 us (2%)
    convert_element_type x1, other arithmetic, local(): hyena_out = (hyena_inputs[0].astype(jnp.float32) * (skip_bias[None, :] *...  140 us
    ppermute x8, waiting for transfers between devices, shifted_2(): return lax.ppermute(shard, axis, pairs)  81.1 us
    ppermute x8, starting transfers between devices, shifted_2(): return lax.ppermute(shard, axis, pairs)  18.6 us
    concatenate x10, other arithmetic, local(): extended = jnp.concatenate([left_rim, kv_product], axis=0)  14.2 us
    all_to_all x1, starting transfers between devices, local(): lax.all_to_all(filters.astype(jnp.bfloat16), 'tp', split_axis=1, concat_a...  9.38 us
  transfers between devices with their start and end apart: 9, of which 6 were waited for; matrix products, arithmetic and copies ran while one was open for 58% of the time, Pallas kernels for 0%

commit v1 on v0

v1 whole, which is shorter than its diff:
```python
import functools
import math

import jax
import jax.numpy as jnp
from jax import lax
from jax.experimental import pallas as pl
from jax.experimental.pallas import tpu as pltpu
from jax.sharding import PartitionSpec as P

MESH = pl.DeviceIdType.MESH
HD = 128
FLEN = 128
HOPS = 7
ROW = 4
BLK = 128
SHIFTS = 8


def kernel(
    ctx_count,
    tp_count,
    hy_ref,
    filt_ref,
    bias_ref,
    q_ref,
    kv_ref,
    ds_ref,
    hy_out,
    att_out,
    lt_out,
    kvb,
    qb,
    dsb,
    hyv,
    filtv,
    filtb,
    tapb,
    taps,
    halo,
    prod,
    xw,
    xs,
    ob,
    lts,
    ltr,
    send,
    recv,
    local,
):
    ctx = lax.axis_index("ctx")
    tp = lax.axis_index("tp")
    x = ctx % ROW
    row = ctx // ROW
    row_count = ctx_count // ROW
    up = ((row + 1) % row_count) * ROW + x
    down = ((row + row_count - 1) % row_count) * ROW + x
    after = (ctx + 1) % ctx_count
    before = (ctx + ctx_count - 1) % ctx_count
    ch = hy_ref.shape[2]
    wide = q_ref.shape[1] // ROW
    own_heads = wide // HD
    tap_rows = filt_ref.shape[0]

    def mate(d):
        return row * ROW + (x + d) % ROW

    barrier = pltpu.get_barrier_semaphore()
    peers = [(mate(d), tp) for d in (1, 2, 3)] + [(up, tp), (down, tp), (after, tp), (before, tp)]
    peers += [(ctx, (tp + d) % tp_count) for d in range(1, tp_count)]
    for peer in peers:
        pl.semaphore_signal(barrier, inc=1, device_id=peer, device_id_type=MESH)

    copies = {}

    def remote(name, src, dst, peer):
        index = len(copies)
        copies[name] = pltpu.make_async_remote_copy(
            src_ref=src,
            dst_ref=dst,
            send_sem=send.at[index],
            recv_sem=recv.at[index],
            device_id=peer,
            device_id_type=MESH,
        )
        return copies[name]

    filt_in = pltpu.make_async_copy(filt_ref, filtv, local.at[0])
    hy_in = pltpu.make_async_copy(hy_ref, hyv, local.at[1])
    kv_in = pltpu.make_async_copy(
        kv_ref.at[:, :, pl.ds(pl.multiple_of(x * wide, wide), wide)], kvb.at[8 + x], local.at[2]
    )
    q_in = pltpu.make_async_copy(
        q_ref.at[:, pl.ds(pl.multiple_of(x * wide, wide), wide)], qb.at[x], local.at[3]
    )
    ds_in = pltpu.make_async_copy(ds_ref, dsb.at[x], local.at[4])
    filt_in.start()
    hy_in.start()
    ds_in.start()
    kv_in.start()
    q_in.start()
    pl.semaphore_wait(barrier, len(peers))

    own_cols = pl.ds(pl.multiple_of(x * wide, wide), wide)
    remote(("y1", 0), kv_ref.at[:, :, own_cols], kvb.at[4 + x], (up, tp)).start()
    for d in (1, 3, 2):
        cols = pl.ds(pl.multiple_of(((x + d) % ROW) * wide, wide), wide)
        remote(("kv", d), kv_ref.at[:, :, cols], kvb.at[8 + x], (mate(d), tp)).start()
    filt_in.wait()
    filtb[...] = filtv[...].astype(jnp.bfloat16)
    for d in range(1, tp_count):
        other = (tp + d) % tp_count
        cols = pl.ds(pl.multiple_of(other * ch, ch), ch)
        rows = pl.ds(pl.multiple_of(tp * tap_rows, tap_rows), tap_rows)
        remote(("tap", d), filtb.at[:, cols], tapb.at[rows], (ctx, other)).start()
    tap_in = pltpu.make_async_copy(
        filtb.at[:, pl.ds(pl.multiple_of(tp * ch, ch), ch)],
        tapb.at[pl.ds(pl.multiple_of(tp * tap_rows, tap_rows), tap_rows)],
        local.at[5],
    )
    tap_in.start()
    for d in (1, 3, 2):
        cols = pl.ds(pl.multiple_of(((x + d) % ROW) * wide, wide), wide)
        remote(("q", d), q_ref.at[:, cols], qb.at[x], (mate(d), tp)).start()
        remote(("ds", d), ds_ref, dsb.at[x], (mate(d), tp)).start()
    hy_in.wait()
    product = (hyv[1].astype(jnp.float32) * hyv[2].astype(jnp.float32)).astype(jnp.bfloat16)
    prod[...] = product
    remote(("halo", 0), prod, halo, (after, tp)).start()
    xw[pl.ds(BLK, BLK), :] = product.astype(jnp.float32)

    for d in (1, 3, 2):
        copies[("kv", d)].wait_recv()
        slot = (x + ROW - d) % ROW
        remote(("y1", d), kvb.at[8 + slot], kvb.at[4 + slot], (up, tp)).start()

    hops = (0, 1, 3, 2)

    def forward(d):
        copies[("y1", d)].wait_recv()
        slot = (x + ROW - d) % ROW
        onward = remote(("y2", d), kvb.at[4 + slot], kvb.at[slot], (up, tp))

        @pl.when(slot != 0)
        def _():
            onward.start()

    forward(0)

    copies[("halo", 0)].wait_recv()
    xw[pl.ds(0, BLK), :] = halo[...].astype(jnp.float32)
    for b in range(SHIFTS):
        xs[b, pl.ds(8, 2 * BLK - 8), :] = xw[pl.ds(8 - b, 2 * BLK - 8), :]
    forward(1)
    tap_in.wait()
    for d in range(1, tp_count):
        copies[("tap", d)].wait_recv()
    taps[...] = tapb[...].astype(jnp.float32)
    ds_in.wait()
    base = row * ROW * BLK

    def columns_of(i):
        starts = (dsb[i] - base).astype(jnp.float32)
        return jnp.broadcast_to(starts, (BLK, BLK)).T

    place = lax.broadcasted_iota(jnp.int32, (BLK, BLK), 0).astype(jnp.float32)
    reach = place + (x * BLK).astype(jnp.float32) - columns_of(x)

    def conv_tile(c, carry):
        lanes = pl.ds(pl.multiple_of(c * 128, 128), 128)

        def group(a, acc):
            first = pl.multiple_of(BLK - 8 * a, 8)
            group_taps = taps[pl.ds(pl.multiple_of(8 * a, 8), 8), lanes]
            for b in range(SHIFTS):
                lag = 8 * a + b
                term = xs[b, pl.ds(first, BLK), lanes] * group_taps[b : b + 1]
                acc = acc + jnp.where(reach >= lag.astype(jnp.float32), term, 0.0)
            return acc

        acc = lax.fori_loop(0, FLEN // SHIFTS, group, jnp.zeros((BLK, 128), jnp.float32))
        acc = bias_ref[:, lanes] * xw[pl.ds(BLK, BLK), lanes] + acc
        hy_out[:, lanes] = (hyv[0, :, lanes].astype(jnp.float32) * acc).astype(jnp.bfloat16)
        return carry

    lax.fori_loop(0, ch // 256, conv_tile, 0)
    forward(3)
    lax.fori_loop(ch // 256, ch // 128, conv_tile, 0)
    forward(2)

    kv_in.wait()
    q_in.wait()
    for d in (1, 2, 3):
        copies[("q", d)].wait_recv()
        copies[("ds", d)].wait_recv()
    for d in hops:
        slot = (x + ROW - d) % ROW

        @pl.when(slot != 0)
        def _():
            copies[("y2", d)].wait_recv()

    scale = 1.0 / math.sqrt(HD)
    span = (HOPS + 1) * BLK
    for d in (1, 2, 3, 0):
        i = (x + d) % ROW
        starts = jnp.concatenate([columns_of(i)] * (HOPS + 1), axis=1)
        keys_at = lax.broadcasted_iota(jnp.int32, (BLK, span), 1).astype(jnp.float32) + (
            (i - HOPS) * BLK
        ).astype(jnp.float32)
        queries_at = lax.broadcasted_iota(jnp.int32, (BLK, span), 0).astype(jnp.float32) + (
            i * BLK
        ).astype(jnp.float32)
        allowed = (keys_at >= starts) & (keys_at <= queries_at)
        for h in range(own_heads):
            cols = pl.ds(h * HD, HD)
            queries = qb[i, :, cols]
            keys = kvb[pl.ds(i + 1, HOPS + 1), 0, :, cols].reshape(span, HD)
            values = kvb[pl.ds(i + 1, HOPS + 1), 1, :, cols].reshape(span, HD)
            scores = (
                lax.dot_general(
                    queries, keys, (((1,), (1,)), ((), ())), preferred_element_type=jnp.float32
                )
                * scale
            )
            scores = jnp.where(allowed, scores, -1e30)
            top = jnp.max(scores, axis=1, keepdims=True)
            weights = jnp.exp(scores - top)
            total = jnp.sum(weights, axis=1, keepdims=True)
            mixed = jnp.dot(
                weights.astype(jnp.bfloat16), values, preferred_element_type=jnp.float32
            )
            ob[d, :, cols] = (mixed / total).astype(jnp.bfloat16)
            logs = jnp.broadcast_to(top + jnp.log(total), (BLK, BLK)).T
            lts[d, pl.ds(h, 1), :] = logs[0:1, :]
        mine = att_out.at[:, own_cols]
        if d:
            remote(("o", d), ob.at[d], mine, (mate(d), tp)).start()
            remote(("lt", d), lts.at[d], ltr.at[x], (mate(d), tp)).start()
        else:
            o_in = pltpu.make_async_copy(ob.at[0], mine, local.at[6])
            o_in.start()
            ltr[x] = lts[0]
    o_in.wait()
    for d in (1, 2, 3):
        copies[("o", d)].wait_recv()
        copies[("lt", d)].wait_recv()
    for s in range(ROW):
        lt_out[pl.ds(s * own_heads, own_heads), :] = ltr[s, pl.ds(0, own_heads), :]
    for name, copy in copies.items():
        if name[0] == "y2":
            slot = (x + ROW - name[1]) % ROW

            @pl.when(slot != 0)
            def _():
                copy.wait_send()
        else:
            copy.wait_send()


def local_part(ctx_count, tp_count, hyena_inputs, filters, skip_bias, queries, keys_values, doc_start):
    rows, ch = queries.shape
    heads = ch // HD
    wide = ch // ROW
    hbm = pl.BlockSpec(memory_space=pl.ANY)
    vmem = pl.BlockSpec(memory_space=pltpu.VMEM)
    bf16, f32 = jnp.bfloat16, jnp.float32
    return pl.pallas_call(
        functools.partial(kernel, ctx_count, tp_count),
        name="row_exchange",
        out_shape=(
            jax.ShapeDtypeStruct((rows, ch), bf16),
            jax.ShapeDtypeStruct((rows, ch), bf16),
            jax.ShapeDtypeStruct((heads, rows), f32),
        ),
        in_specs=[hbm, hbm, vmem, hbm, hbm, hbm],
        out_specs=(vmem, hbm, vmem),
        scratch_shapes=[
            pltpu.VMEM((3 * ROW, 2, BLK, wide), bf16),
            pltpu.VMEM((ROW, BLK, wide), bf16),
            pltpu.VMEM((ROW, 1, BLK), jnp.int32),
            pltpu.VMEM((3, BLK, ch), bf16),
            pltpu.VMEM(filters.shape, f32),
            pltpu.VMEM(filters.shape, bf16),
            pltpu.VMEM((FLEN, ch), bf16),
            pltpu.VMEM((FLEN, ch), f32),
            pltpu.VMEM((BLK, ch), bf16),
            pltpu.VMEM((BLK, ch), bf16),
            pltpu.VMEM((2 * BLK, ch), f32),
            pltpu.VMEM((SHIFTS, 2 * BLK, ch), f32),
            pltpu.VMEM((ROW, BLK, wide), bf16),
            pltpu.VMEM((ROW, 8, BLK), f32),
            pltpu.VMEM((ROW, 8, BLK), f32),
            pltpu.SemaphoreType.DMA((32,)),
            pltpu.SemaphoreType.DMA((32,)),
            pltpu.SemaphoreType.DMA((8,)),
        ],
        compiler_params=pltpu.CompilerParams(
            collective_id=0, has_side_effects=True, vmem_limit_bytes=48 * 2**20
        ),
    )(hyena_inputs, filters, skip_bias.reshape(1, ch), queries, keys_values, doc_start.reshape(1, rows))


def solution(mesh):
    in_specs = (
        P(None, "ctx", "tp"),
        P("tp", None),
        P("tp"),
        P("ctx", "tp"),
        P(None, "ctx", "tp"),
        P("ctx"),
    )
    out_specs = (P("ctx", "tp"), P("ctx", "tp"), P("tp", "ctx"))
    part = functools.partial(local_part, mesh.shape["ctx"], mesh.shape["tp"])
    return jax.shard_map(part, mesh=mesh, in_specs=in_specs, out_specs=out_specs, check_vma=False)
```

time: 280 us -> 73.7 us (0.26)
  the two profiles are of different devices: /device:TPU:64 before, /device:TPU:202 now
where the time goes in v1:
time: 73.7 us; the launch traced here: 73.4 us
  Pallas kernels  65.2 us (88%)
  local copies, waits for them, and re-layouts  7.5 us (10%)
    pallas_call x1, Pallas kernels, local_part(): pl.pallas_call(functools.partial(kernel, ctx_count, tp_count), name='row_...  65.2 us
    unnamed x15, local copies, waits for them, and re-layouts  7.5 us

profile of v1, /device:TPU:202, one launch (start us, length us, event | category | flops | bytes accessed | tf_op | source)
XLA Modules:
  0.0 73.4 jit_solution(5186852082915248044)
XLA Ops:
  0.6 0.0 copy-start.5
  0.6 0.6 copy-done.5
  1.3 0.0 copy-start
  1.3 1.1 %copy-done = bf16[3,128,1024]{2,1,0:T(8,128)(2,1)S(1)} copy-done((bf16[3,128,1024]{2,1,0:T(8,128)(2,1)S(1)}, bf16[3,128,1024]{2,1,0:T(8,128)(2,1)}, u32[]{:S(2)}) %copy-start) | copy-done | bytes 786456
  2.4 0.0 copy-start.1
  2.4 1.0 %copy-done.1 = f32[32,4096]{1,0:T(8,128)S(1)} copy-done((f32[32,4096]{1,0:T(8,128)S(1)}, f32[32,4096]{1,0:T(8,128)}, u32[]{:S(2)}) %copy-start.1) | copy-done | bytes 524312
  3.5 0.0 copy-start.2
  3.5 1.0 %copy-done.2 = bf16[2,128,1024]{2,1,0:T(8,128)(2,1)S(1)} copy-done((bf16[2,128,1024]{2,1,0:T(8,128)(2,1)S(1)}, bf16[2,128,1024]{2,1,0:T(8,128)(2,1)}, u32[]{:S(2)}) %copy-start.2) | copy-done | bytes 524312
  4.5 0.0 copy-start.3
  4.5 0.9 %copy-done.3 = bf16[128,1024]{1,0:T(8,128)(2,1)S(1)} copy-done((bf16[128,1024]{1,0:T(8,128)(2,1)S(1)}, bf16[128,1024]{1,0:T(8,128)(2,1)}, u32[]{:S(2)}) %copy-start.3) | copy-done | bytes 262168
  5.5 0.0 copy-start.4
  5.5 0.7 copy-done.4
  6.1 65.2 %row_exchange.1 = (bf16[128,1024]{1,0:T(8,128)(2,1)S(1)}, bf16[128,1024]{1,0:T(8,128)(2,1)S(1)}, f32[8,128]{1,0:T(8,128)S(1)}) custom-call(bf16[3,128,1024]{2,1,0:T(8,128)(2,1)S(1)} %copy-done, f32[32,4096]{1,0:T(8,128)S(1)} %copy-done.1, f32[1,1024]{1,0:T(1,128)S(1)} %bitcast.2, bf16[128,1024]{1,0:T(8,128)(2,1)S(1)} %copy-done.3, ...), custom_call_target="tpu_custom_call" | custom-call | tf_op jit(solution)/shard_map/row_exchange/pallas_call | solution.py:268
  71.4 0.7 copy.12
  72.1 0.7 copy.13
  72.8 0.6 copy.14
Async XLA Ops:
  0.6 0.7 copy-start.5
  1.3 1.1 %copy-start = (bf16[3,128,1024]{2,1,0:T(8,128)(2,1)S(1)}, bf16[3,128,1024]{2,1,0:T(8,128)(2,1)}, u32[]{:S(2)}) copy-start(bf16[3,128,1024]{2,1,0:T(8,128)(2,1)} %hy_ref.1) | copy-start | bytes 2359300
  2.4 1.0 %copy-start.1 = (f32[32,4096]{1,0:T(8,128)S(1)}, f32[32,4096]{1,0:T(8,128)}, u32[]{:S(2)}) copy-start(f32[32,4096]{1,0:T(8,128)} %filt_ref.1) | copy-start | bytes 1572868
  3.5 1.0 %copy-start.2 = (bf16[2,128,1024]{2,1,0:T(8,128)(2,1)S(1)}, bf16[2,128,1024]{2,1,0:T(8,128)(2,1)}, u32[]{:S(2)}) copy-start(bf16[2,128,1024]{2,1,0:T(8,128)(2,1)} %kv_ref.1) | copy-start | bytes 1572868
  4.5 0.9 %copy-start.3 = (bf16[128,1024]{1,0:T(8,128)(2,1)S(1)}, bf16[128,1024]{1,0:T(8,128)(2,1)}, u32[]{:S(2)}) copy-start(bf16[128,1024]{1,0:T(8,128)(2,1)} %q_ref.1) | copy-start | bytes 786436
  5.5 0.7 copy-start.4

commit v2 on v1

v2 whole, which is shorter than its diff:
```python
import functools
import math

import jax
import jax.numpy as jnp
from jax import lax
from jax.experimental import pallas as pl
from jax.experimental.pallas import tpu as pltpu
from jax.sharding import PartitionSpec as P

MESH = pl.DeviceIdType.MESH
HD = 128
FLEN = 128
ROW = 4
BLK = 128
HEADS = 2
SHIFTS = 8
FAR = ROW - 1
NONE = -1e30


def kernel(
    ctx_count,
    tp_count,
    hy_ref,
    filt_ref,
    bias_ref,
    q_ref,
    kv_ref,
    ds_ref,
    hy_out,
    att_out,
    lt_out,
    kvb,
    qb,
    dsb,
    o2s,
    o2r,
    l2s,
    l2r,
    o1s,
    o1r,
    l1s,
    l1r,
    o1p,
    l1p,
    o0p,
    l0p,
    ob,
    lts,
    ltr,
    hyv,
    filtv,
    filtb,
    tapb,
    taps,
    halo,
    prod,
    xw,
    xs,
    send,
    recv,
    local,
):
    ctx = lax.axis_index("ctx")
    tp = lax.axis_index("tp")
    x = ctx % ROW
    row = ctx // ROW
    row_count = ctx_count // ROW
    has_up = row < row_count - 1
    has_up2 = row < row_count - 2
    has_down = row > 0
    up = ((row + 1) % row_count) * ROW + x
    down = ((row + row_count - 1) % row_count) * ROW + x
    after = (ctx + 1) % ctx_count
    before = (ctx + ctx_count - 1) % ctx_count
    ch = hy_ref.shape[2]
    tap_rows = filt_ref.shape[0]
    bf16, f32 = jnp.bfloat16, jnp.float32

    def mate(d):
        return row * ROW + (x + d) % ROW

    def head_cols(owner, h):
        return pl.ds(pl.multiple_of((owner * HEADS + h) * HD, HD), HD)

    barrier = pltpu.get_barrier_semaphore()
    peers = [(mate(d), tp) for d in (1, 2, 3)] + [(up, tp), (down, tp), (after, tp), (before, tp)]
    peers += [(ctx, (tp + d) % tp_count) for d in range(1, tp_count)]
    for peer in peers:
        pl.semaphore_signal(barrier, inc=1, device_id=peer, device_id_type=MESH)

    copies = {}
    sending = {}

    def remote(name, src, dst, peer, when=None):
        index = len(copies)
        copy = pltpu.make_async_remote_copy(
            src_ref=src,
            dst_ref=dst,
            send_sem=send.at[index],
            recv_sem=recv.at[index],
            device_id=peer,
            device_id_type=MESH,
        )
        copies[name] = copy
        sending[name] = when
        if when is None:
            copy.start()
        else:
            pl.when(when)(copy.start)

    def arrived(name, when=None):
        if when is None:
            copies[name].wait_recv()
        else:
            pl.when(when)(copies[name].wait_recv)

    filt_in = pltpu.make_async_copy(filt_ref, filtv, local.at[0])
    hy_in = pltpu.make_async_copy(hy_ref, hyv, local.at[1])
    ds_in = pltpu.make_async_copy(ds_ref, dsb.at[0, x], local.at[2])
    q_in = [
        pltpu.make_async_copy(q_ref.at[:, head_cols(x, h)], qb.at[h, 0, x], local.at[3 + h])
        for h in range(HEADS)
    ]
    kv_in = [
        pltpu.make_async_copy(kv_ref.at[:, :, head_cols(x, h)], kvb.at[h, x], local.at[5 + h])
        for h in range(HEADS)
    ]
    filt_in.start()
    for copy in q_in:
        copy.start()
    ds_in.start()
    hy_in.start()
    for copy in kv_in:
        copy.start()

    @pl.when(row == 0)
    def _():
        o2r[...] = jnp.zeros_like(o2r)
        o1r[...] = jnp.zeros_like(o1r)
        l2r[...] = jnp.full_like(l2r, NONE)
        l1r[...] = jnp.full_like(l1r, NONE)

    @pl.when(ctx == 0)
    def _():
        halo[...] = jnp.zeros_like(halo)

    pl.semaphore_wait(barrier, len(peers))

    for h in range(HEADS):
        for d in (1, 3, 2):
            cols = head_cols((x + d) % ROW, h)
            remote(("q", h, d), q_ref.at[:, cols], qb.at[h, 0, x], (mate(d), tp))
    for d in (1, 3, 2):
        remote(("ds", d), ds_ref, dsb.at[0, x], (mate(d), tp))
    filt_in.wait()
    filtb[...] = filtv[...].astype(bf16)
    own_taps = pl.ds(pl.multiple_of(tp * tap_rows, tap_rows), tap_rows)
    for d in range(1, tp_count):
        other = (tp + d) % tp_count
        cols = pl.ds(pl.multiple_of(other * ch, ch), ch)
        remote(("tap", d), filtb.at[:, cols], tapb.at[own_taps], (ctx, other))
    tap_in = pltpu.make_async_copy(
        filtb.at[:, pl.ds(pl.multiple_of(tp * ch, ch), ch)], tapb.at[own_taps], local.at[7]
    )
    tap_in.start()
    for h in range(HEADS):
        for d in (1, 3, 2):
            cols = head_cols((x + d) % ROW, h)
            remote(("kv", h, d), kv_ref.at[:, :, cols], kvb.at[h, x], (mate(d), tp))

    ds_in.wait()
    for d in (1, 3, 2):
        arrived(("ds", d))
    remote("ds1", dsb.at[0], dsb.at[1], (down, tp), has_down)
    for h in range(HEADS):
        q_in[h].wait()
        for d in (1, 3, 2):
            arrived(("q", h, d))
        remote(("q1", h), qb.at[h, 0], qb.at[h, 1], (down, tp), has_down)

    hy_in.wait()
    product = (hyv[1].astype(f32) * hyv[2].astype(f32)).astype(bf16)
    prod[...] = product
    has_after = ctx < ctx_count - 1
    has_before = ctx > 0
    remote("halo", prod, halo, (after, tp), has_after)
    xw[pl.ds(BLK, BLK), :] = product.astype(f32)

    both = has_down & has_up
    arrived("ds1", has_up)
    remote("ds2", dsb.at[1], dsb.at[2], (down, tp), both)
    for h in range(HEADS):
        arrived(("q1", h), has_up)
        remote(
            ("q2", h),
            qb.at[h, 1, pl.ds(0, FAR)],
            qb.at[h, 2, pl.ds(0, FAR)],
            (down, tp),
            both,
        )

    base = row * ROW * BLK
    scale = 1.0 / math.sqrt(HD)

    def attend(h, level, first):
        count = FAR if level == 2 else ROW
        span = (ROW - first) * BLK
        keys = kvb[h, pl.ds(first, ROW - first), 0].reshape(span, HD)
        values = kvb[h, pl.ds(first, ROW - first), 1].reshape(span, HD)
        queries = qb[h, level, pl.ds(0, count)].reshape(count * BLK, HD)
        scores = lax.dot_general(
            keys, queries, (((1,), (1,)), ((), ())), preferred_element_type=f32
        )
        starts = jnp.concatenate([dsb[level, i] for i in range(count)], axis=1) - base
        places = lax.broadcasted_iota(jnp.int32, scores.shape, 0) + first * BLK
        allowed = places >= starts
        if level == 0:
            allowed = allowed & (places <= lax.broadcasted_iota(jnp.int32, scores.shape, 1))
        scores = jnp.where(allowed, scores * scale, NONE)
        top = jnp.max(scores, axis=0, keepdims=True)
        weights = jnp.exp(scores - top)
        total = jnp.sum(weights, axis=0, keepdims=True)
        mixed = lax.dot_general(
            values, weights.astype(bf16), (((0,), (0,)), ((), ())), preferred_element_type=f32
        )
        return mixed / total, top + jnp.log(total)

    def merged(mixed_a, logs_a, mixed_b, logs_b):
        top = jnp.maximum(logs_a, logs_b)
        share_a = jnp.exp(logs_a - top)
        share_b = jnp.exp(logs_b - top)
        total = share_a + share_b
        mixed = mixed_a * (share_a / total) + mixed_b * (share_b / total)
        return mixed, top + jnp.log(total)

    def far_part(h):
        arrived(("q2", h), has_up2)

        @pl.when(has_up2)
        def _():
            mixed, logs = attend(h, 2, 1)
            o2s[h] = mixed.astype(bf16)
            l2s[h] = logs

        remote(("o2", h), o2s.at[h], o2r.at[h], (up, tp), has_up2)
        remote(("l2", h), l2s.at[h], l2r.at[h], (up, tp), has_up2)

    def near_part(h):
        @pl.when(has_up)
        def _():
            mixed, logs = attend(h, 1, 0)
            o1p[h] = mixed
            l1p[h] = logs

    def own_part(h):
        mixed, logs = attend(h, 0, 0)
        o0p[h] = mixed
        l0p[h] = logs

    def pass_on(h):
        came = both
        arrived(("o2", h), came)
        arrived(("l2", h), came)

        @pl.when(has_up)
        def _():
            far, far_logs = o2r[h].astype(f32), l2r[h]
            cut = FAR * BLK
            mixed, logs = merged(o1p[h, :, pl.ds(0, cut)], l1p[h, :, pl.ds(0, cut)], far, far_logs)
            o1s[h, :, pl.ds(0, cut)] = mixed.astype(bf16)
            l1s[h, :, pl.ds(0, cut)] = logs
            o1s[h, :, pl.ds(cut, BLK)] = o1p[h, :, pl.ds(cut, BLK)].astype(bf16)
            l1s[h, :, pl.ds(cut, BLK)] = l1p[h, :, pl.ds(cut, BLK)]

        remote(("o1", h), o1s.at[h], o1r.at[h], (up, tp), has_up)
        remote(("l1", h), l1s.at[h], l1r.at[h], (up, tp), has_up)

    def finish(h):
        arrived(("o1", h), has_down)
        arrived(("l1", h), has_down)
        mixed, logs = merged(o0p[h], l0p[h], o1r[h].astype(f32), l1r[h])
        for i in range(ROW):
            ob[h, i] = mixed[:, i * BLK : (i + 1) * BLK].T.astype(bf16)
            lts[h, i] = logs[:, i * BLK : (i + 1) * BLK]
        for d in (1, 3, 2):
            to = (x + d) % ROW
            remote(("o", h, d), ob.at[h, to], att_out.at[:, head_cols(x, h)], (mate(d), tp))
            remote(("lt", h, d), lts.at[h, to], ltr.at[h, x], (mate(d), tp))
        att_out[:, head_cols(x, h)] = ob[h, x]
        ltr[h, x] = lts[h, x]

    def conv_tile(c, carry):
        lanes = pl.ds(pl.multiple_of(c * 128, 128), 128)
        starts = jnp.broadcast_to((dsb[0, x] - base).astype(f32), (BLK, BLK)).T
        place = lax.broadcasted_iota(jnp.int32, (BLK, BLK), 0).astype(f32)
        reach = place + (x * BLK).astype(f32) - starts

        def group(a, acc):
            first = pl.multiple_of(BLK - 8 * a, 8)
            group_taps = taps[pl.ds(pl.multiple_of(8 * a, 8), 8), lanes]
            for b in range(SHIFTS):
                lag = 8 * a + b
                term = xs[b, pl.ds(first, BLK), lanes] * group_taps[b : b + 1]
                acc = acc + jnp.where(reach >= lag.astype(f32), term, 0.0)
            return acc

        acc = lax.fori_loop(0, FLEN // SHIFTS, group, jnp.zeros((BLK, 128), f32))
        acc = bias_ref[:, lanes] * xw[pl.ds(BLK, BLK), lanes] + acc
        hy_out[:, lanes] = (hyv[0, :, lanes].astype(f32) * acc).astype(bf16)
        return carry

    tiles = ch // 128

    def convolve(first, last):
        lax.fori_loop(first, last, conv_tile, 0)

    arrived("ds2", has_up2)
    for h in range(HEADS):
        kv_in[h].wait()
        for d in (1, 3, 2):
            arrived(("kv", h, d))
        far_part(h)
        near_part(h)
    for h in range(HEADS):
        own_part(h)
    tap_in.wait()
    for d in range(1, tp_count):
        arrived(("tap", d))
    taps[...] = tapb[...].astype(f32)
    arrived("halo", has_before)
    xw[pl.ds(0, BLK), :] = halo[...].astype(f32)
    for b in range(SHIFTS):
        xs[b, pl.ds(8, 2 * BLK - 8), :] = xw[pl.ds(8 - b, 2 * BLK - 8), :]
    pass_on(0)
    convolve(0, tiles // 4)
    pass_on(1)
    convolve(tiles // 4, tiles // 2)
    finish(0)
    convolve(tiles // 2, 3 * tiles // 4)
    finish(1)
    convolve(3 * tiles // 4, tiles)
    for h in range(HEADS):
        for d in (1, 3, 2):
            arrived(("o", h, d))
            arrived(("lt", h, d))
    for s in range(ROW):
        for h in range(HEADS):
            lt_out[pl.ds(s * HEADS + h, 1), :] = ltr[h, s]
    for name, copy in copies.items():
        if sending[name] is None:
            copy.wait_send()
        else:
            pl.when(sending[name])(copy.wait_send)


def local_part(ctx_count, tp_count, hyena_inputs, filters, skip_bias, queries, keys_values, doc_start):
    rows, ch = queries.shape
    heads = ch // HD
    wide = ROW * BLK
    hbm = pl.BlockSpec(memory_space=pl.ANY)
    vmem = pl.BlockSpec(memory_space=pltpu.VMEM)
    bf16, f32 = jnp.bfloat16, jnp.float32
    return pl.pallas_call(
        functools.partial(kernel, ctx_count, tp_count),
        name="row_exchange",
        out_shape=(
            jax.ShapeDtypeStruct((rows, ch), bf16),
            jax.ShapeDtypeStruct((rows, ch), bf16),
            jax.ShapeDtypeStruct((heads, rows), f32),
        ),
        in_specs=[hbm, hbm, vmem, hbm, hbm, hbm],
        out_specs=(vmem, vmem, vmem),
        scratch_shapes=[
            pltpu.VMEM((HEADS, ROW, 2, BLK, HD), bf16),
            pltpu.VMEM((HEADS, 3, ROW, BLK, HD), bf16),
            pltpu.VMEM((3, ROW, 1, BLK), jnp.int32),
            pltpu.VMEM((HEADS, HD, FAR * BLK), bf16),
            pltpu.VMEM((HEADS, HD, FAR * BLK), bf16),
            pltpu.VMEM((HEADS, 1, FAR * BLK), f32),
            pltpu.VMEM((HEADS, 1, FAR * BLK), f32),
            pltpu.VMEM((HEADS, HD, wide), bf16),
            pltpu.VMEM((HEADS, HD, wide), bf16),
            pltpu.VMEM((HEADS, 1, wide), f32),
            pltpu.VMEM((HEADS, 1, wide), f32),
            pltpu.VMEM((HEADS, HD, wide), f32),
            pltpu.VMEM((HEADS, 1, wide), f32),
            pltpu.VMEM((HEADS, HD, wide), f32),
            pltpu.VMEM((HEADS, 1, wide), f32),
            pltpu.VMEM((HEADS, ROW, BLK, HD), bf16),
            pltpu.VMEM((HEADS, ROW, 1, BLK), f32),
            pltpu.VMEM((HEADS, ROW, 1, BLK), f32),
            pltpu.VMEM((3, BLK, ch), bf16),
            pltpu.VMEM(filters.shape, f32),
            pltpu.VMEM(filters.shape, bf16),
            pltpu.VMEM((FLEN, ch), bf16),
            pltpu.VMEM((FLEN, ch), f32),
            pltpu.VMEM((BLK, ch), bf16),
            pltpu.VMEM((BLK, ch), bf16),
            pltpu.VMEM((2 * BLK, ch), f32),
            pltpu.VMEM((SHIFTS, 2 * BLK, ch), f32),
            pltpu.SemaphoreType.DMA((48,)),
            pltpu.SemaphoreType.DMA((48,)),
            pltpu.SemaphoreType.DMA((8,)),
        ],
        compiler_params=pltpu.CompilerParams(
            collective_id=0, has_side_effects=True, vmem_limit_bytes=63 * 2**20
        ),
    )(hyena_inputs, filters, skip_bias.reshape(1, ch), queries, keys_values, doc_start.reshape(1, rows))


def solution(mesh):
    in_specs = (
        P(None, "ctx", "tp"),
        P("tp", None),
        P("tp"),
        P("ctx", "tp"),
        P(None, "ctx", "tp"),
        P("ctx"),
    )
    out_specs = (P("ctx", "tp"), P("ctx", "tp"), P("tp", "ctx"))
    part = functools.partial(local_part, mesh.shape["ctx"], mesh.shape["tp"])
    return jax.shard_map(part, mesh=mesh, in_specs=in_specs, out_specs=out_specs, check_vma=False)
```

time: 73.7 us -> 53.4 us (0.72)
  the two profiles are of different devices: /device:TPU:202 before, /device:TPU:16 now
where the time goes in v2:
time: 53.4 us; the launch traced here: 53.2 us
  Pallas kernels  49.5 us (93%)
  local copies, waits for them, and re-layouts  3.01 us (6%)
  between operations  0.65 us (1%)
    pallas_call x1, Pallas kernels, local_part(): pl.pallas_call(functools.partial(kernel, ctx_count, tp_count), name='row_...  49.5 us
    unnamed x7, local copies, waits for them, and re-layouts  3.01 us

profile of v2, /device:TPU:16, one launch (start us, length us, event | category | flops | bytes accessed | tf_op | source)
XLA Modules:
  0.0 53.2 jit_solution(4105051764308353931)
XLA Ops:
  0.6 49.5 %row_exchange.1 = (bf16[128,1024]{1,0:T(8,128)(2,1)}, bf16[128,1024]{1,0:T(8,128)(2,1)}, f32[8,128]{1,0:T(8,128)}) custom-call(bf16[3,128,1024]{2,1,0:T(8,128)(2,1)} %hy_ref.1, f32[32,4096]{1,0:T(8,128)} %filt_ref.1, f32[1,1024]{1,0:T(1,128)} %bitcast.2, bf16[128,1024]{1,0:T(8,128)(2,1)} %q_ref.1, bf16[2,128,1024]{2,1,0:T(8,128)(2,1)} %kv_ref.1, ...), custom_call_target="tpu_custom_call" | custom-call | tf_op jit(solution)/shard_map/row_exchange/pallas_call | solution.py:365
  50.2 0.0 copy-start
  50.2 1.7 %copy.12 = bf16[128,1024]{1,0:T(8,128)(2,1)} copy(bf16[128,1024]{1,0:T(8,128)(2,1)} %get-tuple-element.6) | data formatting | bytes 524288
  51.9 0.0 copy-done
  51.9 0.0 copy-start.1
  51.9 0.7 %copy.13 = bf16[128,1024]{1,0:T(8,128)(2,1)} copy(bf16[128,1024]{1,0:T(8,128)(2,1)S(1)} %copy-done) | data formatting | bytes 524288
  52.6 0.0 copy-done.1
  52.6 0.6 %copy.14 = f32[8,128]{1,0:T(8,128)} copy(f32[8,128]{1,0:T(8,128)S(1)} %copy-done.1) | data formatting | bytes 8192
Async XLA Ops:
  50.2 1.7 %copy-start = (bf16[128,1024]{1,0:T(8,128)(2,1)S(1)}, bf16[128,1024]{1,0:T(8,128)(2,1)}, u32[]{:S(2)}) copy-start(bf16[128,1024]{1,0:T(8,128)(2,1)} %get-tuple-element.7) | copy-start | bytes 786436
  51.9 0.7 %copy-start.1 = (f32[8,128]{1,0:T(8,128)S(1)}, f32[8,128]{1,0:T(8,128)}, u32[]{:S(2)}) copy-start(f32[8,128]{1,0:T(8,128)} %get-tuple-element.8) | copy-start | bytes 12292

commit v3 on v2

v3 whole, which is shorter than its diff:
```python
import functools
import math

import jax
import jax.numpy as jnp
from jax import lax
from jax.experimental import pallas as pl
from jax.experimental.pallas import tpu as pltpu
from jax.sharding import PartitionSpec as P

MESH = pl.DeviceIdType.MESH
HD = 128
FLEN = 128
ROW = 4
BLK = 128
CORES = 2
PLANES = 4
PARTNER = (2, 1, 3, 0)
HEADS = 2
SHIFTS = 8
NONE = -1e30
NOTE = 16


def kernel(
    ctx_count,
    tp_count,
    hy_ref,
    filt_ref,
    bias_ref,
    q_ref,
    kv_ref,
    ds_ref,
    hy_out,
    att_out,
    lt_out,
    kvb,
    qb,
    dsb,
    sent,
    came,
    hyv,
    filtv,
    filtb,
    tapb,
    taps,
    halo,
    prod,
    early,
    late,
    earlys,
    lates,
    convolved,
    biasv,
    send,
    recv,
    local,
    ready,
):
    ctx = lax.axis_index("ctx")
    tp = lax.axis_index("tp")
    x = ctx % ROW
    row = ctx // ROW
    row_count = ctx_count // ROW
    plane = ctx_count // PLANES
    has_up = row < row_count - 1
    has_down = row > 0
    up = ((row + 1) % row_count) * ROW + x
    down = ((row + row_count - 1) % row_count) * ROW + x
    after = (ctx + 1) % ctx_count
    ch = hy_ref.shape[2]
    tap_rows = filt_ref.shape[0]
    bf16, f32 = jnp.bfloat16, jnp.float32

    def mate(d):
        return row * ROW + (x + d) % ROW

    def head_cols(owner, h):
        return pl.ds(pl.multiple_of((owner * HEADS + h) * HD, HD), HD)

    level = ctx // plane
    low = tp < CORES
    partner = 0
    for mine in range(PLANES):
        theirs = jnp.where(low, PARTNER[mine], PARTNER.index(mine))
        partner = jnp.where(level == mine, theirs, partner)
    mirrored = partner * plane + ctx % plane

    def holder(other):
        return jnp.where(other // CORES == tp // CORES, ctx, mirrored)

    def higher(d):
        return ((row + 1) % row_count) * ROW + (x + d) % ROW

    def lower(d):
        return ((row + row_count - 1) % row_count) * ROW + (x + d) % ROW

    barrier = pltpu.get_barrier_semaphore()

    def greet(peer):
        pl.semaphore_signal(barrier, inc=1, device_id=peer, device_id_type=MESH)

    for d in range(1, ROW):
        greet((mate(d), tp))
    for other in range(1, tp_count):

        @pl.when(other > tp)
        def _():
            greet((holder(other), other))

    @pl.when(has_up)
    def _():
        for d in range(ROW):
            greet((higher(d), tp))

    @pl.when(has_down)
    def _():
        for d in range(ROW):
            greet((lower(d), tp))

    greetings = ROW - 1 + tp + ROW * (has_up.astype(jnp.int32) + has_down.astype(jnp.int32))

    copies = {}
    sending = {}

    def remote(name, src, dst, peer, when=None):
        index = len(copies)
        copy = pltpu.make_async_remote_copy(
            src_ref=src,
            dst_ref=dst,
            send_sem=send.at[index],
            recv_sem=recv.at[index],
            device_id=peer,
            device_id_type=MESH,
        )
        copies[name] = copy
        sending[name] = when
        if when is None:
            copy.start()
        else:
            pl.when(when)(copy.start)

    def arrived(name, when=None):
        if when is None:
            copies[name].wait_recv()
        else:
            pl.when(when)(copies[name].wait_recv)

    filt_in = pltpu.make_async_copy(filt_ref, filtv, local.at[0])
    hy_in = pltpu.make_async_copy(hy_ref, hyv, local.at[1])
    ds_in = pltpu.make_async_copy(ds_ref, dsb.at[0, x], local.at[2])
    q_in = [
        pltpu.make_async_copy(q_ref.at[:, head_cols(x, h)], qb.at[h, 0, x], local.at[3 + h])
        for h in range(HEADS)
    ]
    kv_in = [
        pltpu.make_async_copy(kv_ref.at[:, :, head_cols(x, h)], kvb.at[h, ROW + x], local.at[5 + h])
        for h in range(HEADS)
    ]
    filt_in.start()
    for copy in q_in:
        copy.start()
    ds_in.start()
    hy_in.start()
    bias_in = pltpu.make_async_copy(bias_ref, biasv, local.at[8])
    bias_in.start()
    for copy in kv_in:
        copy.start()

    @pl.when(row == 0)
    def _():
        note = lax.broadcasted_iota(jnp.int32, (NOTE, BLK), 0)
        for h in range(HEADS):
            for s in range(ROW):
                came[1, h, s, pl.ds(0, HD), :] = jnp.zeros((HD, BLK), bf16)
                came[1, h, s, pl.ds(HD, NOTE), :] = jnp.where(note == 0, NONE, 0.0).astype(bf16)
        for h in range(HEADS):
            kvb[h, pl.ds(0, ROW)] = jnp.zeros((ROW, 2, BLK, HD), bf16)

    @pl.when(ctx == 0)
    def _():
        halo[...] = jnp.zeros_like(halo)

    pl.semaphore_wait(barrier, greetings)
    for other in range(tp_count - 1):

        @pl.when(other < tp)
        def _():
            pl.semaphore_signal(
                ready.at[tp], inc=1, device_id=(holder(other), other), device_id_type=MESH
            )

    def slot(d):
        return (x + ROW - d) % ROW

    def send_queries(h):
        for d in (1, 3, 2):
            cols = head_cols((x + d) % ROW, h)
            remote(("q", h, d), q_ref.at[:, cols], qb.at[h, 0, x], (mate(d), tp))
        remote(("qd", h, 0), q_ref.at[:, head_cols(x, h)], qb.at[h, 1, x], (down, tp), has_down)

    def send_keys(h):
        for d in (1, 3, 2):
            cols = head_cols((x + d) % ROW, h)
            remote(("kv", h, d), kv_ref.at[:, :, cols], kvb.at[h, ROW + x], (mate(d), tp))
        remote(
            ("ku", h, 0),
            kv_ref.at[:, :, head_cols(x, h)],
            kvb.at[h, x],
            (up, tp),
            has_up & (x != 0),
        )

    def queries_down(h, d):
        arrived(("q", h, d))
        remote(("qd", h, d), qb.at[h, 0, slot(d)], qb.at[h, 1, slot(d)], (down, tp), has_down)

    def keys_up(h, d):
        arrived(("kv", h, d))
        remote(
            ("ku", h, d),
            kvb.at[h, ROW + slot(d)],
            kvb.at[h, slot(d)],
            (up, tp),
            has_up & (slot(d) != 0),
        )

    send_queries(0)
    send_keys(0)
    for d in (1, 3, 2):
        remote(("ds", d), ds_ref, dsb.at[0, x], (mate(d), tp))
    filt_in.wait()
    filtb[...] = filtv[...].astype(bf16)
    own_taps = pl.ds(pl.multiple_of(tp * tap_rows, tap_rows), tap_rows)
    for d in range(1, tp_count):
        other = (tp + d) % tp_count
        cols = pl.ds(pl.multiple_of(other * ch, ch), ch)
        remote(("tap", d), filtb.at[:, cols], tapb.at[own_taps], (holder(other), other), other < tp)
        sending[("tap", d)] = None
    tap_in = pltpu.make_async_copy(
        filtb.at[:, pl.ds(pl.multiple_of(tp * ch, ch), ch)], tapb.at[own_taps], local.at[7]
    )
    tap_in.start()
    for d in (1, 3, 2):
        queries_down(0, d)
    ds_in.wait()
    for d in (1, 3, 2):
        arrived(("ds", d))
    remote("ds1", dsb.at[0], dsb.at[1], (down, tp), has_down)
    keys_up(0, 1)
    keys_up(0, 3)
    send_queries(1)
    keys_up(0, 2)
    send_keys(1)

    hy_in.wait()
    product = (hyv[1].astype(f32) * hyv[2].astype(f32)).astype(bf16)
    prod[...] = product
    late[pl.ds(0, SHIFTS), :] = jnp.zeros((SHIFTS, ch), f32)
    late[pl.ds(SHIFTS, BLK), :] = product.astype(f32)
    for b in range(SHIFTS):
        lates[b] = late[pl.ds(SHIFTS - b, BLK), :]

    for d in (1, 3, 2):
        queries_down(1, d)
    for d in (1, 3, 2):
        keys_up(1, d)
    for d in range(1, tp_count):
        other = (tp + d) % tp_count

        @pl.when(other > tp)
        def _():
            pl.semaphore_wait(ready.at[other], 1)
            copies[("tap", d)].start()

    remote("halo", prod, halo, (after, tp), ctx < ctx_count - 1)

    base = row * ROW * BLK
    scale = 1.0 / math.sqrt(HD)

    def attend(h, level, first):
        span = (2 * ROW - first) * BLK
        keys = kvb[h, pl.ds(first, 2 * ROW - first), 0].reshape(span, HD)
        values = kvb[h, pl.ds(first, 2 * ROW - first), 1].reshape(span, HD)
        queries = qb[h, level].reshape(ROW * BLK, HD)
        scores = lax.dot_general(
            keys, queries, (((1,), (1,)), ((), ())), preferred_element_type=f32
        )
        starts = jnp.concatenate([dsb[level, i] for i in range(ROW)], axis=1) - base
        places = lax.broadcasted_iota(jnp.int32, scores.shape, 0) + (first - ROW) * BLK
        allowed = places >= starts
        if level == 0:
            allowed = allowed & (places <= lax.broadcasted_iota(jnp.int32, scores.shape, 1))
        scores = jnp.where(allowed, scores * scale, NONE)
        top = jnp.max(scores, axis=0, keepdims=True)
        weights = jnp.exp(scores - top)
        total = jnp.sum(weights, axis=0, keepdims=True)
        mixed = lax.dot_general(
            values, weights.astype(bf16), (((0,), (0,)), ((), ())), preferred_element_type=f32
        )
        return mixed / total, top + jnp.log(total)

    def merged(mixed_a, logs_a, mixed_b, logs_b):
        top = jnp.maximum(logs_a, logs_b)
        share_a = jnp.exp(logs_a - top)
        share_b = jnp.exp(logs_b - top)
        total = share_a + share_b
        mixed = mixed_a * (share_a / total) + mixed_b * (share_b / total)
        return mixed, top + jnp.log(total)

    def stage(level, h, mixed, logs):
        first = logs.astype(bf16).astype(f32)
        second = (logs - first).astype(bf16).astype(f32)
        third = logs - first - second
        place = lax.broadcasted_iota(jnp.int32, (NOTE, BLK), 0)
        for i in range(ROW):
            cols = slice(i * BLK, (i + 1) * BLK)
            sent[level, h, i, pl.ds(0, HD), :] = mixed[:, cols].astype(bf16)
            terms = jnp.where(
                place == 0,
                first[:, cols],
                jnp.where(place == 1, second[:, cols], jnp.where(place == 2, third[:, cols], 0.0)),
            )
            sent[level, h, i, pl.ds(HD, NOTE), :] = terms.astype(bf16)

    def own_part(h):
        q_in[h].wait()
        kv_in[h].wait()
        stage(0, h, *attend(h, 0, ROW))
        for d in (1, 3, 2):
            to = (x + d) % ROW
            remote(("o0", h, d), sent.at[0, h, to], came.at[0, h, x], (mate(d), tp))
        came[0, h, x] = sent[0, h, x]

    def earlier_part(h):
        for d in range(ROW):
            arrived(("qd", h, d), has_up)
            arrived(("ku", h, d), has_down & (slot(d) != 0))

        @pl.when(has_up)
        def _():
            stage(1, h, *attend(h, 1, 1))

        for d in (0, 1, 3, 2):
            to = (x + d) % ROW
            remote(("o1", h, d), sent.at[1, h, to], came.at[1, h, x], (higher(d), tp), has_up)

    def finish(h, s):
        own, earlier = came[0, h, s], came[1, h, s]

        def logs_of(tile):
            note = tile[HD:].astype(f32)
            return note[0:1] + note[1:2] + note[2:3]

        mixed, logs = merged(
            own[:HD].astype(f32), logs_of(own), earlier[:HD].astype(f32), logs_of(earlier)
        )
        head = s * HEADS + h
        att_out[:, pl.ds(head * HD, HD)] = mixed.T.astype(bf16)
        lt_out[pl.ds(head, 1), :] = logs

    groups = BLK // SHIFTS

    def reach_tiles():
        starts = jnp.broadcast_to((dsb[0, x] - base).astype(f32), (BLK, BLK)).T
        place = lax.broadcasted_iota(jnp.int32, (BLK, BLK), 0).astype(f32)
        reach = place + (x * BLK).astype(f32) - starts
        return [reach[SHIFTS * k : SHIFTS * (k + 1)] for k in range(groups)]

    def add_taps(acc, source, lanes, first_of, last_of, row_of):
        reach = reach_tiles()
        for a in range(groups):
            group_taps = taps[pl.ds(SHIFTS * a, SHIFTS), lanes]
            for b in range(SHIFTS):
                weight = jnp.broadcast_to(group_taps[b : b + 1], (SHIFTS, BLK))
                for k in range(first_of(a), last_of(a)):
                    term = source[b, pl.ds(SHIFTS * row_of(k, a), SHIFTS), lanes] * weight
                    acc[k] = acc[k] + jnp.where(reach[k] >= SHIFTS * a + b, term, 0.0)

    def late_tile(c, carry):
        lanes = pl.ds(pl.multiple_of(c * 128, 128), 128)
        acc = [jnp.zeros((SHIFTS, 128), f32) for _ in range(groups)]
        add_taps(acc, lates, lanes, lambda a: a, lambda a: groups, lambda k, a: k - a)
        for k in range(groups):
            convolved[pl.ds(SHIFTS * k, SHIFTS), lanes] = acc[k]
        return carry

    def early_tile(c, carry):
        lanes = pl.ds(pl.multiple_of(c * 128, 128), 128)
        acc = [convolved[pl.ds(SHIFTS * k, SHIFTS), lanes] for k in range(groups)]
        add_taps(acc, earlys, lanes, lambda a: 0, lambda a: a + 1, lambda k, a: groups + k - a)
        total = jnp.concatenate(acc, axis=0)
        total = biasv[:, lanes] * late[pl.ds(SHIFTS, BLK), lanes] + total
        hy_out[:, lanes] = (hyv[0, :, lanes].astype(f32) * total).astype(bf16)
        return carry

    tiles = ch // 128

    own_part(0)
    own_part(1)
    tap_in.wait()
    for d in range(1, tp_count):
        arrived(("tap", d))
    taps[...] = tapb[...].astype(f32)
    arrived("ds1", has_up)
    lax.fori_loop(0, tiles // 2, late_tile, 0)
    earlier_part(0)
    lax.fori_loop(tiles // 2, tiles, late_tile, 0)
    earlier_part(1)
    arrived("halo", ctx > 0)
    early[pl.ds(0, BLK), :] = halo[...].astype(f32)
    early[pl.ds(BLK, SHIFTS), :] = jnp.zeros((SHIFTS, ch), f32)
    for b in range(SHIFTS):
        earlys[b, pl.ds(SHIFTS, BLK), :] = early[pl.ds(SHIFTS - b, BLK), :]
    bias_in.wait()
    lax.fori_loop(0, tiles, early_tile, 0)
    for h in range(HEADS):
        for d in (1, 3, 2):
            arrived(("o0", h, d))
        for d in (0, 1, 3, 2):
            arrived(("o1", h, d), has_down)
        for s in range(ROW):
            finish(h, s)
    for name, copy in copies.items():
        if sending[name] is None:
            copy.wait_send()
        else:
            pl.when(sending[name])(copy.wait_send)


def local_part(ctx_count, tp_count, hyena_inputs, filters, skip_bias, queries, keys_values, doc_start):
    rows, ch = queries.shape
    heads = ch // HD
    hbm = pl.BlockSpec(memory_space=pltpu.HBM)
    vmem = pl.BlockSpec(memory_space=pltpu.VMEM)

    def in_hbm(array):
        return pltpu.with_memory_space_constraint(array, pltpu.HBM)

    bf16, f32 = jnp.bfloat16, jnp.float32
    return pl.pallas_call(
        functools.partial(kernel, ctx_count, tp_count),
        name="row_exchange",
        out_shape=(
            jax.ShapeDtypeStruct((rows, ch), bf16),
            jax.ShapeDtypeStruct((rows, ch), bf16),
            jax.ShapeDtypeStruct((heads, rows), f32),
        ),
        in_specs=[hbm] * 6,
        out_specs=(vmem, vmem, vmem),
        scratch_shapes=[
            pltpu.VMEM((HEADS, 2 * ROW, 2, BLK, HD), bf16),
            pltpu.VMEM((HEADS, 2, ROW, BLK, HD), bf16),
            pltpu.VMEM((2, ROW, 1, BLK), jnp.int32),
            pltpu.VMEM((2, HEADS, ROW, HD + NOTE, BLK), bf16),
            pltpu.VMEM((2, HEADS, ROW, HD + NOTE, BLK), bf16),
            pltpu.VMEM((3, BLK, ch), bf16),
            pltpu.VMEM(filters.shape, f32),
            pltpu.VMEM(filters.shape, bf16),
            pltpu.VMEM((FLEN, ch), bf16),
            pltpu.VMEM((FLEN, ch), f32),
            pltpu.VMEM((BLK, ch), bf16),
            pltpu.VMEM((BLK, ch), bf16),
            pltpu.VMEM((BLK + SHIFTS, ch), f32),
            pltpu.VMEM((SHIFTS + BLK, ch), f32),
            pltpu.VMEM((SHIFTS, BLK + SHIFTS, ch), f32),
            pltpu.VMEM((SHIFTS, BLK, ch), f32),
            pltpu.VMEM((BLK, ch), f32),
            pltpu.VMEM((1, ch), f32),
            pltpu.SemaphoreType.DMA((56,)),
            pltpu.SemaphoreType.DMA((56,)),
            pltpu.SemaphoreType.DMA((9,)),
            pltpu.SemaphoreType.REGULAR((tp_count,)),
        ],
        compiler_params=pltpu.CompilerParams(
            collective_id=0, has_side_effects=True, vmem_limit_bytes=40 * 2**20
        ),
    )(
        in_hbm(hyena_inputs),
        in_hbm(filters),
        in_hbm(skip_bias.reshape(1, ch)),
        in_hbm(queries),
        in_hbm(keys_values),
        in_hbm(doc_start.reshape(1, rows)),
    )


def solution(mesh):
    in_specs = (
        P(None, "ctx", "tp"),
        P("tp", None),
        P("tp"),
        P("ctx", "tp"),
        P(None, "ctx", "tp"),
        P("ctx"),
    )
    out_specs = (P("ctx", "tp"), P("ctx", "tp"), P("tp", "ctx"))
    part = functools.partial(local_part, mesh.shape["ctx"], mesh.shape["tp"])
    return jax.shard_map(part, mesh=mesh, in_specs=in_specs, out_specs=out_specs, check_vma=False)
```

time: 53.4 us -> 42.5 us (0.80)
  the two profiles are of different devices: /device:TPU:16 before, /device:TPU:64 now
where the time goes in v3:
time: 42.5 us; the launch traced here: 42.4 us
  Pallas kernels  39.7 us (93%)
  local copies, waits for them, and re-layouts  2 us (5%)
  between operations  0.64 us (2%)
    pallas_call x1, Pallas kernels, local_part(): pl.pallas_call(functools.partial(kernel, ctx_count, tp_count), name='row_...  39.7 us
    unnamed x3, local copies, waits for them, and re-layouts  2 us

profile of v3, /device:TPU:64, one launch (start us, length us, event | category | flops | bytes accessed | tf_op | source)
XLA Modules:
  0.0 42.4 jit_solution(14870016580927821323)
XLA Ops:
  0.6 39.7 %row_exchange.1 = (bf16[128,1024]{1,0:T(8,128)(2,1)S(1)}, bf16[128,1024]{1,0:T(8,128)(2,1)S(1)}, f32[8,128]{1,0:T(8,128)S(1)}) custom-call(bf16[3,128,1024]{2,1,0:T(8,128)(2,1)} %hy_ref.1, f32[32,4096]{1,0:T(8,128)} %filt_ref.1, f32[1,1024]{1,0:T(1,128)} %bitcast.2, bf16[128,1024]{1,0:T(8,128)(2,1)} %q_ref.1, bf16[2,128,1024]{2,1,0:T(8,128)(2,1)} %kv_ref.1, ...), custom_call_target="tpu_custom_call" | custom-call | tf_op jit(solution)/shard_map/row_exchange/pallas_call | solution.py:441
  40.4 0.7 %copy.12 = bf16[128,1024]{1,0:T(8,128)(2,1)} copy(bf16[128,1024]{1,0:T(8,128)(2,1)S(1)} %get-tuple-element.6) | data formatting | bytes 524288
  41.1 0.7 %copy.13 = bf16[128,1024]{1,0:T(8,128)(2,1)} copy(bf16[128,1024]{1,0:T(8,128)(2,1)S(1)} %get-tuple-element.7) | data formatting | bytes 524288
  41.8 0.6 %copy.14 = f32[8,128]{1,0:T(8,128)} copy(f32[8,128]{1,0:T(8,128)S(1)} %get-tuple-element.8) | data formatting | bytes 8192

commit v4 on v3

--- a/solution.py
+++ b/solution.py
@@ -225,6 +225,16 @@
             has_up & (slot(d) != 0),
         )
 
+    def late_taps(sibling):
+        for d in range(1, tp_count):
+            other = (tp + d) % tp_count
+            here = (other // CORES == tp // CORES) == sibling
+
+            @pl.when((other > tp) & here)
+            def _():
+                pl.semaphore_wait(ready.at[other], 1)
+                copies[("tap", d)].start()
+
     send_queries(0)
     send_keys(0)
     for d in (1, 3, 2):
@@ -252,6 +262,7 @@
     send_queries(1)
     keys_up(0, 2)
     send_keys(1)
+    late_taps(True)
 
     hy_in.wait()
     product = (hyv[1].astype(f32) * hyv[2].astype(f32)).astype(bf16)
@@ -265,14 +276,7 @@
         queries_down(1, d)
     for d in (1, 3, 2):
         keys_up(1, d)
-    for d in range(1, tp_count):
-        other = (tp + d) % tp_count
-
-        @pl.when(other > tp)
-        def _():
-            pl.semaphore_wait(ready.at[other], 1)
-            copies[("tap", d)].start()
-
+    late_taps(False)
     remote("halo", prod, halo, (after, tp), ctx < ctx_count - 1)
 
     base = row * ROW * BLK
@@ -361,54 +365,96 @@
 
     groups = BLK // SHIFTS
 
+    def start_columns():
+        return jnp.broadcast_to((dsb[0, x] - base).astype(f32), (BLK, BLK)).T
+
+    def rows_at():
+        return lax.broadcasted_iota(jnp.int32, (BLK, BLK), 0).astype(f32) + (x * BLK).astype(f32)
+
     def reach_tiles():
-        starts = jnp.broadcast_to((dsb[0, x] - base).astype(f32), (BLK, BLK)).T
-        place = lax.broadcasted_iota(jnp.int32, (BLK, BLK), 0).astype(f32)
-        reach = place + (x * BLK).astype(f32) - starts
+        reach = rows_at() - start_columns()
         return [reach[SHIFTS * k : SHIFTS * (k + 1)] for k in range(groups)]
 
-    def add_taps(acc, source, lanes, first_of, last_of, row_of):
-        reach = reach_tiles()
-        for a in range(groups):
+    def add_taps(acc, source, lanes, lag_groups, rows_of, row_of, reach):
+        for a in lag_groups:
             group_taps = taps[pl.ds(SHIFTS * a, SHIFTS), lanes]
             for b in range(SHIFTS):
                 weight = jnp.broadcast_to(group_taps[b : b + 1], (SHIFTS, BLK))
-                for k in range(first_of(a), last_of(a)):
+                for k in rows_of(a):
                     term = source[b, pl.ds(SHIFTS * row_of(k, a), SHIFTS), lanes] * weight
-                    acc[k] = acc[k] + jnp.where(reach[k] >= SHIFTS * a + b, term, 0.0)
-
-    def late_tile(c, carry):
+                    if reach is not None:
+                        term = jnp.where(reach[k] >= SHIFTS * a + b, term, 0.0)
+                    acc[k] = acc[k] + term
+
+    def late_terms(half, fresh):
+        def tile(c, carry):
+            lanes = pl.ds(pl.multiple_of(c * 128, 128), 128)
+            rows = [pl.ds(SHIFTS * k, SHIFTS) for k in range(groups)]
+            if fresh:
+                acc = [jnp.zeros((SHIFTS, 128), f32) for _ in rows]
+            else:
+                acc = [convolved[r, lanes] for r in rows]
+            lag_groups = range(half * groups // 2, (half + 1) * groups // 2)
+            reach = reach_tiles()
+            add_taps(
+                acc, lates, lanes, lag_groups, lambda a: range(a, groups), lambda k, a: k - a, reach
+            )
+            for k, r in enumerate(rows):
+                if fresh or k >= lag_groups[0]:
+                    convolved[r, lanes] = acc[k]
+            return carry
+
+        lax.fori_loop(0, tiles, tile, 0)
+
+    def late_pass(halves, fresh):
+        for half in range(2):
+            which = (tp // CORES == half) == halves
+
+            @pl.when(which)
+            def _():
+                late_terms(half, fresh)
+
+    def tap_half(half):
+        rows = pl.ds(pl.multiple_of(half * FLEN // 2, FLEN // 2), FLEN // 2)
+        taps[rows, :] = tapb[rows, :].astype(f32)
+
+    def early_tile(c, carry):
         lanes = pl.ds(pl.multiple_of(c * 128, 128), 128)
         acc = [jnp.zeros((SHIFTS, 128), f32) for _ in range(groups)]
-        add_taps(acc, lates, lanes, lambda a: a, lambda a: groups, lambda k, a: k - a)
-        for k in range(groups):
-            convolved[pl.ds(SHIFTS * k, SHIFTS), lanes] = acc[k]
-        return carry
-
-    def early_tile(c, carry):
-        lanes = pl.ds(pl.multiple_of(c * 128, 128), 128)
-        acc = [convolved[pl.ds(SHIFTS * k, SHIFTS), lanes] for k in range(groups)]
-        add_taps(acc, earlys, lanes, lambda a: 0, lambda a: a + 1, lambda k, a: groups + k - a)
-        total = jnp.concatenate(acc, axis=0)
+        add_taps(
+            acc, earlys, lanes, range(groups), lambda a: range(a + 1), lambda k, a: groups + k - a, None
+        )
+        reaches_back = start_columns() < (x * BLK).astype(f32)
+        total = jnp.where(reaches_back, jnp.concatenate(acc, axis=0), 0.0)
+        total = convolved[:, lanes] + total
         total = biasv[:, lanes] * late[pl.ds(SHIFTS, BLK), lanes] + total
         hy_out[:, lanes] = (hyv[0, :, lanes].astype(f32) * total).astype(bf16)
         return carry
 
     tiles = ch // 128
 
+    even = tp % CORES == 0
+    tap_in.wait()
+    pl.when(even)(copies[("tap", 3)].wait_recv)
+    pl.when(jnp.logical_not(even))(copies[("tap", 1)].wait_recv)
+    tap_half(tp // CORES)
+    late_pass(True, True)
     own_part(0)
     own_part(1)
-    tap_in.wait()
-    for d in range(1, tp_count):
-        arrived(("tap", d))
-    taps[...] = tapb[...].astype(f32)
     arrived("ds1", has_up)
-    lax.fori_loop(0, tiles // 2, late_tile, 0)
     earlier_part(0)
-    lax.fori_loop(tiles // 2, tiles, late_tile, 0)
     earlier_part(1)
+    arrived(("tap", 2))
+    pl.when(even)(copies[("tap", 1)].wait_recv)
+    pl.when(jnp.logical_not(even))(copies[("tap", 3)].wait_recv)
+    tap_half(1 - tp // CORES)
+    late_pass(False, False)
     arrived("halo", ctx > 0)
-    early[pl.ds(0, BLK), :] = halo[...].astype(f32)
+    first_start = start_columns()[0:1]
+    for c in range(tiles):
+        cols = slice(c * 128, (c + 1) * 128)
+        within = rows_at() - BLK >= first_start
+        early[pl.ds(0, BLK), cols] = jnp.where(within, halo[:, cols].astype(f32), 0.0)
     early[pl.ds(BLK, SHIFTS), :] = jnp.zeros((SHIFTS, ch), f32)
     for b in range(SHIFTS):
         earlys[b, pl.ds(SHIFTS, BLK), :] = early[pl.ds(SHIFTS - b, BLK), :]

time: 42.5 us -> 41.1 us (0.967)
  the two profiles are of different devices: /device:TPU:64 before, /device:TPU:130 now
where the time goes in v4:
time: 41.1 us; the launch traced here: 41 us
  Pallas kernels  38.3 us (93%)
  local copies, waits for them, and re-layouts  2 us (5%)
  between operations  0.64 us (2%)
    pallas_call x1, Pallas kernels, local_part(): pl.pallas_call(functools.partial(kernel, ctx_count, tp_count), name='row_...  38.3 us
    unnamed x3, local copies, waits for them, and re-layouts  2 us

profile of v4, /device:TPU:130, one launch (start us, length us, event | category | flops | bytes accessed | tf_op | source)
XLA Modules:
  0.0 41.0 jit_solution(7140886154409089075)
XLA Ops:
  0.6 38.3 %row_exchange.1 = (bf16[128,1024]{1,0:T(8,128)(2,1)S(1)}, bf16[128,1024]{1,0:T(8,128)(2,1)S(1)}, f32[8,128]{1,0:T(8,128)S(1)}) custom-call(bf16[3,128,1024]{2,1,0:T(8,128)(2,1)} %hy_ref.1, f32[32,4096]{1,0:T(8,128)} %filt_ref.1, f32[1,1024]{1,0:T(1,128)} %bitcast.2, bf16[128,1024]{1,0:T(8,128)(2,1)} %q_ref.1, bf16[2,128,1024]{2,1,0:T(8,128)(2,1)} %kv_ref.1, ...), custom_call_target="tpu_custom_call" | custom-call | tf_op jit(solution)/shard_map/row_exchange/pallas_call | solution.py:487
  39.0 0.7 %copy.12 = bf16[128,1024]{1,0:T(8,128)(2,1)} copy(bf16[128,1024]{1,0:T(8,128)(2,1)S(1)} %get-tuple-element.6) | data formatting | bytes 524288
  39.7 0.7 %copy.13 = bf16[128,1024]{1,0:T(8,128)(2,1)} copy(bf16[128,1024]{1,0:T(8,128)(2,1)S(1)} %get-tuple-element.7) | data formatting | bytes 524288
  40.4 0.6 %copy.14 = f32[8,128]{1,0:T(8,128)} copy(f32[8,128]{1,0:T(8,128)S(1)} %get-tuple-element.8) | data formatting | bytes 8192

commit v5 on v4

--- a/solution.py
+++ b/solution.py
@@ -277,7 +277,6 @@
     for d in (1, 3, 2):
         keys_up(1, d)
     late_taps(False)
-    remote("halo", prod, halo, (after, tp), ctx < ctx_count - 1)
 
     base = row * ROW * BLK
     scale = 1.0 / math.sqrt(HD)
@@ -433,14 +432,15 @@
 
     tiles = ch // 128
 
+    own_part(0)
+    own_part(1)
+    remote("halo", prod, halo, (after, tp), ctx < ctx_count - 1)
     even = tp % CORES == 0
     tap_in.wait()
     pl.when(even)(copies[("tap", 3)].wait_recv)
     pl.when(jnp.logical_not(even))(copies[("tap", 1)].wait_recv)
     tap_half(tp // CORES)
     late_pass(True, True)
-    own_part(0)
-    own_part(1)
     arrived("ds1", has_up)
     earlier_part(0)
     earlier_part(1)

time: 41.1 us -> 40.2 us (0.978)
  Pallas kernels: 38.3 us -> 37.4 us
    pallas_call x1, Pallas kernels: 38.3 us -> 37.4 us  [local_part(): pl.pallas_call(functools.partial(kernel, ctx_count, tp_count), name='row_...]
where the time goes in v5:
time: 40.2 us; the launch traced here: 40 us
  Pallas kernels  37.4 us (93%)
  local copies, waits for them, and re-layouts  2 us (5%)
  between operations  0.64 us (2%)
    pallas_call x1, Pallas kernels, local_part(): pl.pallas_call(functools.partial(kernel, ctx_count, tp_count), name='row_...  37.4 us
    unnamed x3, local copies, waits for them, and re-layouts  2 us

profile of v5, /device:TPU:130, one launch (start us, length us, event | category | flops | bytes accessed | tf_op | source)
XLA Modules:
  0.0 40.0 jit_solution(7937701645250615507)
XLA Ops:
  0.6 37.4 %row_exchange.1 = (bf16[128,1024]{1,0:T(8,128)(2,1)S(1)}, bf16[128,1024]{1,0:T(8,128)(2,1)S(1)}, f32[8,128]{1,0:T(8,128)S(1)}) custom-call(bf16[3,128,1024]{2,1,0:T(8,128)(2,1)} %hy_ref.1, f32[32,4096]{1,0:T(8,128)} %filt_ref.1, f32[1,1024]{1,0:T(1,128)} %bitcast.2, bf16[128,1024]{1,0:T(8,128)(2,1)} %q_ref.1, bf16[2,128,1024]{2,1,0:T(8,128)(2,1)} %kv_ref.1, ...), custom_call_target="tpu_custom_call" | custom-call | tf_op jit(solution)/shard_map/row_exchange/pallas_call | solution.py:487
  38.0 0.7 %copy.12 = bf16[128,1024]{1,0:T(8,128)(2,1)} copy(bf16[128,1024]{1,0:T(8,128)(2,1)S(1)} %get-tuple-element.6) | data formatting | bytes 524288
  38.7 0.7 %copy.13 = bf16[128,1024]{1,0:T(8,128)(2,1)} copy(bf16[128,1024]{1,0:T(8,128)(2,1)S(1)} %get-tuple-element.7) | data formatting | bytes 524288
  39.4 0.6 %copy.14 = f32[8,128]{1,0:T(8,128)} copy(f32[8,128]{1,0:T(8,128)S(1)} %get-tuple-element.8) | data formatting | bytes 8192
